TPU v7x, 32 devices: a whole 2x2x4 slice. The times are simulated.
32 devices in a mesh: pipe: 4 (over y, x), ctx: 8 (over z, core).
Axes of the slice: x: 2, y: 2, z: 4, core: 2. Of those that a mesh axis runs over, the one named last changes fastest.
Arguments:
- queries: bfloat16 [4, 4096, 1024], P('pipe', 'ctx'), may hold values from -14 to 14
- keys: bfloat16 [4, 4096, 128], P('pipe', 'ctx'), may hold values from -14 to 14
- values: bfloat16 [4, 4096, 128], P('pipe', 'ctx'), may hold values from -6 to 6
- out_grad: bfloat16 [4, 4096, 1024], P('pipe', 'ctx'), may hold values from -6 to 6
- doc_lengths: int32 [4, 8], P('pipe'), may hold values from 1 to 2048, 4096 in all within a row
- assignment: int32 [4, 8], P('pipe'), may hold values from 0 to 7, each once within a row
Outputs:
- q_grad_in: bfloat16 [4, 4096, 1024], P('pipe', 'ctx')
- k_grad_in: bfloat16 [4, 4096, 128], P('pipe', 'ctx')
- v_grad_in: bfloat16 [4, 4096, 128], P('pipe', 'ctx')
Inputs may be any that keep to these rules, and one draw needn't show every extreme that they name: Each row is a permutation; device i of ctx holds the blocks assignment[s, i] and 15 - assignment[s, i] of 256 positions, in that order. `doc_lengths`: each row sums to 4096 and its largest entry is 2048.
All inputs are finite; a program needn't handle non-finite values.
Results may differ from a plain program's by a relative error of at most 0.0069.
Values may be sent and summed in bfloat16 or wider, within the bound.
A program may use at most 128 MiB of HBM per device.

v0:
```python
import math

import jax
import jax.numpy as jnp
from jax import lax
from jax.experimental import pallas as pl
from jax.experimental.pallas import tpu as pltpu
from jax.sharding import PartitionSpec as P

masked_score = -1e30


def dot_nt(a, b):
    return lax.dot_general(a, b, (((1,), (1,)), ((), ())), preferred_element_type=jnp.float32)


def dot_nn(a, b):
    return lax.dot_general(a, b, (((1,), (0,)), ((), ())), preferred_element_type=jnp.float32)


def dot_tn(a, b):
    return lax.dot_general(a, b, (((0,), (0,)), ((), ())), preferred_element_type=jnp.float32)


def chip_device(chip, core):
    return {"ctx": 2 * chip + core}


def greet(devices):
    barrier = pltpu.get_barrier_semaphore()
    for there, device in devices:

        @pl.when(there)
        def _():
            pl.semaphore_signal(
                barrier, inc=1, device_id=device, device_id_type=pl.DeviceIdType.MESH
            )

    count = sum(there.astype(jnp.int32) for there, device in devices)
    pl.semaphore_wait(barrier, count)


def remote(source, target, send_sem, recv_sem, device):
    return pltpu.make_async_remote_copy(
        src_ref=source,
        dst_ref=target,
        send_sem=send_sem,
        recv_sem=recv_sem,
        device_id=device,
        device_id_type=pl.DeviceIdType.MESH,
    )


def gather_kernel(
    k_ref,
    v_ref,
    q_ref,
    g_ref,
    kv_ref,
    qo_ref,
    go_ref,
    own_sem,
    line_send,
    line_recv,
    twin_send,
    twin_recv,
    swap_send,
    swap_recv,
):
    me = lax.axis_index("ctx")
    chips = kv_ref.shape[0] // 2
    half = qo_ref.shape[1]
    chip, core = me // 2, me % 2
    twin = chip_device(chip, 1 - core)
    has = (chip < chips - 1, chip > 0)
    ahead = (chip_device(chip + 1, core), chip_device(chip - 1, core))
    always = chip >= 0
    greet([(always, twin), (has[0], ahead[0]), (has[1], ahead[1])])

    sources = (k_ref, v_ref)
    own = [
        pltpu.make_async_copy(ref, kv_ref.at[me, part], own_sem.at[part])
        for part, ref in enumerate(sources)
    ]

    def shard_at(way, step):
        return 2 * (chip - step if way == 0 else chip + step) + core

    def along(way, step, hop, part):
        place = kv_ref.at[shard_at(way, step), part]
        return remote(
            sources[part] if hop == 0 and step == 0 else place,
            place,
            line_send.at[way, hop, part],
            line_recv.at[way, hop, part],
            ahead[way],
        )

    def across(way, step, part):
        place = kv_ref.at[shard_at(way, step), part]
        return remote(
            sources[part] if step == 0 else place,
            place,
            twin_send.at[way, step, part],
            twin_recv.at[way, step, part],
            twin,
        )

    def arriving(way, step):
        return chip - step >= 0 if way == 0 else chip + step < chips

    for part in range(2):
        for way in range(2):

            @pl.when(has[way])
            def _():
                along(way, 0, 0, part).start()

    for part in range(2):
        across(0, 0, part).start()
        own[part].start()
    lanes = pl.ds(pl.multiple_of((1 - core) * half, half), half)
    swaps = [
        remote(q_ref.at[:, lanes], qo_ref, swap_send.at[0], swap_recv.at[0], twin),
        remote(g_ref.at[:, lanes], go_ref, swap_send.at[1], swap_recv.at[1], twin),
    ]
    for copy in swaps:
        copy.start()
    for step in range(1, chips):
        for part in range(2):
            for way in range(2):

                @pl.when(arriving(way, step))
                def _():
                    along(way, step, step - 1, part).wait_recv()

                    @pl.when(has[way])
                    def _():
                        along(way, step, step, part).start()

                    across(way, step, part).start()

    for copy in swaps:
        copy.wait()
    for part in range(2):
        own[part].wait()
        across(0, 0, part).wait()
        for way in range(2):

            @pl.when(has[way])
            def _():
                along(way, 0, 0, part).wait_send()

    for step in range(1, chips):
        for part in range(2):
            for way in range(2):

                @pl.when(arriving(way, step))
                def _():
                    across(way, step, part).wait()

                    @pl.when(has[way])
                    def _():
                        along(way, step, step, part).wait_send()


def gather(keys, values, queries, out_grad):
    rows, width = queries.shape
    n_ctx = lax.axis_size("ctx")
    chips = n_ctx // 2
    half = width // 2
    return pl.pallas_call(
        gather_kernel,
        out_shape=(
            jax.ShapeDtypeStruct((n_ctx, 2) + keys.shape, keys.dtype),
            jax.ShapeDtypeStruct((rows, half), queries.dtype),
            jax.ShapeDtypeStruct((rows, half), queries.dtype),
        ),
        in_specs=[pl.BlockSpec(memory_space=pl.ANY)] * 4,
        out_specs=(pl.BlockSpec(memory_space=pl.ANY),) * 3,
        scratch_shapes=[
            pltpu.SemaphoreType.DMA((2,)),
            pltpu.SemaphoreType.DMA((2, chips, 2)),
            pltpu.SemaphoreType.DMA((2, chips, 2)),
            pltpu.SemaphoreType.DMA((2, chips, 2)),
            pltpu.SemaphoreType.DMA((2, chips, 2)),
            pltpu.SemaphoreType.DMA((2,)),
            pltpu.SemaphoreType.DMA((2,)),
        ],
        compiler_params=pltpu.CompilerParams(collective_id=0, has_side_effects=True),
        name="gather_blocks",
    )(keys, values, queries, out_grad)


def reduce_kernel(
    dq_ref,
    dkv_ref,
    q_in_ref,
    kv_in_ref,
    mine_ref,
    twin_ref,
    line_ref,
    sum_ref,
    twin_send,
    twin_recv,
    line_send,
    line_recv,
    query_send,
    query_recv,
    last_send,
    last_recv,
    mine_sem,
):
    me = lax.axis_index("ctx")
    stage = lax.axis_index("pipe")
    stages = lax.axis_size("pipe")
    chips = dkv_ref.shape[0] // 2
    half = dq_ref.shape[2]
    chip, core = me // 2, me % 2
    twin = chip_device(chip, 1 - core)
    has = (chip < chips - 1, chip > 0)
    ahead = (chip_device(chip + 1, core), chip_device(chip - 1, core))
    always = chip >= 0
    before = lax.rem(stage + stages - 1, stages)
    after = lax.rem(stage + 1, stages)

    def own_part(z):
        return pltpu.make_async_copy(dkv_ref.at[2 * z + core], mine_ref.at[z], mine_sem.at[z])

    order = []
    for z in range(chips // 2):
        order += [z, chips - 1 - z]
    for z in order:
        own_part(z).start()
    greet(
        [(always, twin), (has[0], ahead[0]), (has[1], ahead[1])]
        + [
            (always, {"pipe": other, "ctx": 2 * chip + k})
            for other in (before, after)
            for k in range(2)
        ]
    )

    def crossing(z):
        return remote(
            dkv_ref.at[2 * z + 1 - core], twin_ref.at[z], twin_send.at[z], twin_recv.at[z], twin
        )

    for z in order:
        crossing(z).start()

    lanes = pl.ds(pl.multiple_of(core * half, half), half)

    def query_copy(k, recv_index):
        return remote(
            dq_ref.at[k],
            q_in_ref.at[:, lanes],
            query_send.at[k],
            query_recv.at[recv_index],
            {"pipe": before, "ctx": 2 * chip + k},
        )

    for k in range(2):
        query_copy(k, core).start()

    def passing(way, z, part):
        return remote(
            sum_ref.at[z, part],
            line_ref.at[way, z, part],
            line_send.at[way, z, part],
            line_recv.at[way, z, part],
            ahead[way],
        )

    def add_up(z, part, ways):
        total = mine_ref[z, part].astype(jnp.float32) + twin_ref[z, part].astype(
            jnp.float32
        )
        for way in ways:
            total += line_ref[way, z, part].astype(jnp.float32)
        sum_ref[z, part] = total.astype(sum_ref.dtype)

    for t in range(chips - 1):
        for part in range(2):
            for way in range(2):
                z = chips - 1 - (t - chip) if way == 0 else t - (chips - 1 - chip)
                beyond = (z <= chips - 1) & (z > chip) if way == 0 else (z >= 0) & (z < chip)

                @pl.when(beyond)
                def _():
                    if part == 0:
                        own_part(z).wait()
                        crossing(z).wait_recv()

                    @pl.when(has[1 - way])
                    def _():
                        passing(way, z, part).wait_recv()
                        add_up(z, part, (way,))

                    @pl.when(jnp.logical_not(has[1 - way]))
                    def _():
                        add_up(z, part, ())

                    passing(way, z, part).start()

    own_part(chip).wait()
    crossing(chip).wait_recv()
    lasts = []
    for part in range(2):

        @pl.when(has[0] & has[1])
        def _():
            for way in range(2):
                passing(way, chip, part).wait_recv()
            add_up(chip, part, (0, 1))

        for way in range(2):

            @pl.when(jnp.logical_not(has[way]))
            def _():
                passing(way, chip, part).wait_recv()
                add_up(chip, part, (way,))

        lasts.append(
            remote(
                sum_ref.at[chip, part],
                kv_in_ref.at[part],
                last_send.at[part],
                last_recv.at[part],
                {"pipe": before, "ctx": me},
            )
        )
        lasts[-1].start()
    for k in range(2):
        query_copy(k, k).wait()
    for z in range(chips):
        crossing(z).wait_send()
        for part in range(2):

            @pl.when(z > chip)
            def _():
                passing(0, z, part).wait_send()

            @pl.when(z < chip)
            def _():
                passing(1, z, part).wait_send()

    for copy in lasts:
        copy.wait()


def reduce_and_pass(dq, dkv):
    rows, half = dq.shape[1:]
    n_ctx, _, _, head_width = dkv.shape
    chips = n_ctx // 2
    part = dkv.shape[1:]
    return pl.pallas_call(
        reduce_kernel,
        out_shape=(
            jax.ShapeDtypeStruct((rows, 2 * half), dq.dtype),
            jax.ShapeDtypeStruct((2, rows, head_width), dq.dtype),
        ),
        in_specs=[pl.BlockSpec(memory_space=pl.ANY)] * 2,
        out_specs=(pl.BlockSpec(memory_space=pl.ANY),) * 2,
        scratch_shapes=[
            pltpu.VMEM((chips,) + part, dkv.dtype),
            pltpu.VMEM((chips,) + part, dkv.dtype),
            pltpu.VMEM((2, chips) + part, dkv.dtype),
            pltpu.VMEM((chips,) + part, dkv.dtype),
            pltpu.SemaphoreType.DMA((chips,)),
            pltpu.SemaphoreType.DMA((chips,)),
            pltpu.SemaphoreType.DMA((2, chips, 2)),
            pltpu.SemaphoreType.DMA((2, chips, 2)),
            pltpu.SemaphoreType.DMA((2,)),
            pltpu.SemaphoreType.DMA((2,)),
            pltpu.SemaphoreType.DMA((2,)),
            pltpu.SemaphoreType.DMA((2,)),
            pltpu.SemaphoreType.DMA((chips,)),
        ],
        compiler_params=pltpu.CompilerParams(
            collective_id=1, has_side_effects=True, vmem_limit_bytes=16 * 1024 * 1024
        ),
        name="reduce_and_pass",
    )(dq, dkv)


def attention_kernel(
    sizes_ref,
    placing_ref,
    q_ref,
    g_ref,
    qo_ref,
    go_ref,
    kv_ref,
    dq_ref,
    dkv_ref,
    qs_ref,
    gs_ref,
    s_ref,
    dp_ref,
    top_ref,
    total_ref,
    weighted_ref,
    logsum_ref,
    delta_ref,
    *rest,
):
    low_refs = (rest[:2], rest[2:4])
    dqt_ref, acc_ref, place_ref = rest[4:]
    block = q_ref.shape[0] // 2
    head_width = kv_ref.shape[3]
    head_count = q_ref.shape[1] // head_width
    n_ctx = placing_ref.shape[1]
    n_docs = sizes_ref.shape[1]
    heads = head_count // 2
    wide = heads * block
    scale = 1.0 / math.sqrt(head_width)
    scale2 = scale * math.log2(math.e)
    me = lax.axis_index("ctx")
    chip, core = me // 2, me % 2

    starts = [jnp.int32(0)]
    for d in range(n_docs - 1):
        starts.append(starts[-1] + sizes_ref[0, d])
    for d in range(n_ctx):
        low = placing_ref[0, d]
        place_ref[low] = 2 * d
        place_ref[2 * n_ctx - 1 - low] = 2 * d + 1
    acc_ref[...] = jnp.zeros_like(acc_ref)

    def one_strip(step, carry):
        owner = step // 2
        slot = step % 2
        placed = placing_ref[0, 2 * chip + owner]
        query_block = jnp.where(slot == 0, placed, 2 * n_ctx - 1 - placed)
        rows = pl.ds(pl.multiple_of(slot * block, block), block)

        @pl.when(owner == core)
        def _():
            for h in range(heads):
                lanes = pl.ds(
                    pl.multiple_of((core * heads + h) * head_width, head_width), head_width
                )
                qs_ref[h * block : (h + 1) * block, :] = q_ref[rows, lanes]
                gs_ref[h * block : (h + 1) * block, :] = g_ref[rows, lanes]

        @pl.when(owner != core)
        def _():
            for h in range(heads):
                lanes = slice(h * head_width, (h + 1) * head_width)
                qs_ref[h * block : (h + 1) * block, :] = qo_ref[rows, lanes]
                gs_ref[h * block : (h + 1) * block, :] = go_ref[rows, lanes]

        first = query_block * block
        query_pos = first + lax.broadcasted_iota(jnp.int32, (1, block), 1)
        doc_first = jnp.zeros((1, block), jnp.int32)
        strip_first = jnp.int32(0)
        for start in starts[1:]:
            doc_first = jnp.where(query_pos >= start, start, doc_first)
            strip_first = jnp.where(first >= start, start, strip_first)
        low_block = strip_first // block
        tiles = query_block - low_block + 1
        dqt_ref[...] = jnp.zeros_like(dqt_ref)

        last_doc = jnp.int32(0)
        for start in starts[1:]:
            last_doc = jnp.where(first + block - 1 >= start, start, last_doc)
        top_ref[...] = jnp.full(top_ref.shape, masked_score, jnp.float32)
        total_ref[...] = jnp.zeros_like(total_ref)
        weighted_ref[...] = jnp.zeros_like(weighted_ref)

        def tile_of(t, part):
            stored = place_ref[low_block + t]
            key_rows = pl.ds(pl.multiple_of(stored % 2 * block, block), block)
            return kv_ref[stored // 2, part, key_rows, :]

        def fold(x, combine):
            return combine(x.reshape(block // 8, 8, block), axis=0)

        def forward(tiles_now, masked):
            allowed, key_tiles, value_tiles = [], [], []
            for t in tiles_now:
                key_tiles.append(tile_of(t, 0))
                value_tiles.append(tile_of(t, 1))
                if masked:
                    key_pos = (low_block + t) * block + lax.broadcasted_iota(
                        jnp.int32, (block, block), 0
                    )
                    allowed.append((key_pos <= query_pos) & (key_pos >= doc_first))
            tops = []
            for h in range(heads):
                lanes = slice(h * block, (h + 1) * block)
                top = top_ref[:, lanes]
                for i, t in enumerate(tiles_now):
                    scores = dot_nt(key_tiles[i], qs_ref[lanes, :]) * scale2
                    if masked:
                        scores = jnp.where(allowed[i], scores, masked_score)
                    s_ref[t, :, lanes] = scores
                    top = jnp.maximum(top, jnp.max(fold(scores, jnp.max), axis=0, keepdims=True))
                tops.append(top)
            for h in range(heads):
                lanes = slice(h * block, (h + 1) * block)
                factor = jnp.exp2(top_ref[:, lanes] - tops[h])
                top_ref[:, lanes] = tops[h]
                total = total_ref[:, lanes] * factor
                weighted = weighted_ref[:, lanes] * factor
                for i, t in enumerate(tiles_now):
                    grad_probs = dot_nt(value_tiles[i], gs_ref[lanes, :])
                    dp_ref[t, :, lanes] = grad_probs
                    probs = jnp.exp2(s_ref[t, :, lanes] - tops[h])
                    total += fold(probs, jnp.sum)
                    weighted += fold(probs * grad_probs, jnp.sum)
                total_ref[:, lanes] = total
                weighted_ref[:, lanes] = weighted

        def forward_guarded(tiles_now):
            partial = tiles_now[-1] == tiles - 1
            partial |= (low_block + tiles_now[0]) * block < last_doc

            @pl.when(partial)
            def _():
                forward(tiles_now, True)

            @pl.when(jnp.logical_not(partial))
            def _():
                forward(tiles_now, False)

        def backward(tiles_now):
            for i, t in enumerate(tiles_now):
                stored = place_ref[low_block + t]
                key_rows = pl.ds(pl.multiple_of(stored % 2 * block, block), block)
                key_tile = tile_of(t, 0)
                for h in range(heads):
                    lanes = slice(h * block, (h + 1) * block)
                    for r in range(0, block, 64):
                        softmax = jnp.exp2(s_ref[t, r : r + 64, lanes] - logsum_ref[:, lanes])
                        grad_scores = softmax * (dp_ref[t, r : r + 64, lanes] - delta_ref[:, lanes])
                        low_refs[i][0][r : r + 64, lanes] = softmax.astype(jnp.bfloat16)
                        low_refs[i][1][r : r + 64, lanes] = grad_scores.astype(jnp.bfloat16)
                acc_ref[stored // 2, 1, key_rows, :] += dot_nn(low_refs[i][0][...], gs_ref[...])
                acc_ref[stored // 2, 0, key_rows, :] += dot_nn(low_refs[i][1][...], qs_ref[...])
                dqt_ref[...] += dot_tn(key_tile, low_refs[i][1][...])

        def over_tiles(work):
            def pair(i, carry):
                work([2 * i, 2 * i + 1])
                return carry

            lax.fori_loop(0, tiles // 2, pair, 0)

            @pl.when(tiles % 2 == 1)
            def _():
                work([tiles - 1])

        over_tiles(forward_guarded)
        total = jnp.sum(total_ref[...], axis=0, keepdims=True)
        logsum_ref[...] = top_ref[...] + jnp.log2(total)
        delta_ref[...] = jnp.sum(weighted_ref[...], axis=0, keepdims=True) / total
        over_tiles(backward)
        for h in range(heads):
            dq_ref[owner, rows, h * head_width : (h + 1) * head_width] = (
                jnp.transpose(dqt_ref[:, h * block : (h + 1) * block]) * scale
            ).astype(jnp.bfloat16)
        return carry

    lax.fori_loop(0, 4, one_strip, 0)
    dkv_ref[:, 0] = (acc_ref[:, 0] * scale).astype(dkv_ref.dtype)
    dkv_ref[:, 1] = acc_ref[:, 1].astype(dkv_ref.dtype)


def attention_backward(doc_lengths, assignment, queries, out_grad, queries_other, out_grad_other, kv):
    rows, width = queries.shape
    length = kv.shape[0] * rows
    block = rows // 2
    head_width = kv.shape[3]
    wide = width // head_width // 2 * block
    most = length // 2
    tiles = most // block + 1
    strips = 2 * tiles * block * wide * 4
    limit = strips + 4 * length * head_width * 4 + 20 * rows * width + 6 * 1024 * 1024
    vmem = pl.BlockSpec(memory_space=pltpu.VMEM)
    smem = pl.BlockSpec(memory_space=pltpu.SMEM)
    return pl.pallas_call(
        attention_kernel,
        out_shape=(
            jax.ShapeDtypeStruct((2, rows, width // 2), jnp.bfloat16),
            jax.ShapeDtypeStruct(kv.shape, jnp.bfloat16),
        ),
        in_specs=[smem, smem, vmem, vmem, vmem, vmem, vmem],
        out_specs=(vmem, vmem),
        scratch_shapes=[
            pltpu.VMEM((wide, head_width), jnp.bfloat16),
            pltpu.VMEM((wide, head_width), jnp.bfloat16),
            pltpu.VMEM((tiles, block, wide), jnp.float32),
            pltpu.VMEM((tiles, block, wide), jnp.float32),
            pltpu.VMEM((1, wide), jnp.float32),
            pltpu.VMEM((8, wide), jnp.float32),
            pltpu.VMEM((8, wide), jnp.float32),
            pltpu.VMEM((1, wide), jnp.float32),
            pltpu.VMEM((1, wide), jnp.float32),
            pltpu.VMEM((block, wide), jnp.bfloat16),
            pltpu.VMEM((block, wide), jnp.bfloat16),
            pltpu.VMEM((block, wide), jnp.bfloat16),
            pltpu.VMEM((block, wide), jnp.bfloat16),
            pltpu.VMEM((head_width, wide), jnp.float32),
            pltpu.VMEM(kv.shape, jnp.float32),
            pltpu.SMEM((2 * assignment.shape[1],), jnp.int32),
        ],
        compiler_params=pltpu.CompilerParams(vmem_limit_bytes=limit),
        name="attention_backward",
    )(doc_lengths, assignment, queries, out_grad, queries_other, out_grad_other, kv)


def local(queries, keys, values, out_grad, doc_lengths, assignment):
    kv, queries_other, out_grad_other = gather(keys[0], values[0], queries[0], out_grad[0])
    dq, dkv = attention_backward(
        doc_lengths, assignment, queries[0], out_grad[0], queries_other, out_grad_other, kv
    )
    query_in, kv_in = reduce_and_pass(dq, dkv)
    return query_in[None], kv_in[0][None], kv_in[1][None]


def solution(mesh):
    return jax.shard_map(
        local,
        mesh=mesh,
        in_specs=(
            P("pipe", "ctx", None),
            P("pipe", "ctx", None),
            P("pipe", "ctx", None),
            P("pipe", "ctx", None),
            P("pipe", None),
            P("pipe", None),
        ),
        out_specs=(P("pipe", "ctx", None), P("pipe", "ctx", None), P("pipe", "ctx", None)),
        check_vma=False,
    )
```

profile of v0, /device:TPU:0, one launch (start us, length us, event | category | flops | bytes accessed | tf_op | source)
XLA Modules:
  0.0 82.7 jit_solution(4771447912633592350)
XLA Ops:
  0.6 0.0 copy-start.6
  0.6 0.0 copy-start.5
  0.7 0.0 copy-start.1
  0.7 0.0 copy-start
  0.7 24.5 %gather_blocks.1 = (bf16[8,2,512,128]{3,2,1,0:T(8,128)(2,1)}, bf16[512,512]{1,0:T(8,128)(2,1)}, bf16[512,512]{1,0:T(8,128)(2,1)}) custom-call(bf16[512,128]{1,0:T(8,128)(2,1)} %bitcast.10, bf16[512,128]{1,0:T(8,128)(2,1)} %bitcast.11, bf16[512,1024]{1,0:T(8,128)(2,1)} %bitcast.5, bf16[512,1024]{1,0:T(8,128)(2,1)} %bitcast.7), custom_call_target="tpu_custom_call" | custom-call | tf_op jit(solution)/shard_map/gather_blocks/pallas_call | solution.py:172
  25.2 0.0 copy-done.6
  25.2 0.0 copy-done.5
  25.2 0.0 copy-done.1
  25.2 0.0 copy-done
  25.2 0.0 copy-start.2
  25.3 1.6 %copy-done.2 = bf16[8,2,512,128]{3,2,1,0:T(8,128)(2,1)S(1)} copy-done((bf16[8,2,512,128]{3,2,1,0:T(8,128)(2,1)S(1)}, bf16[8,2,512,128]{3,2,1,0:T(8,128)(2,1)}, u32[]{:S(2)}) %copy-start.2) | copy-done | bytes 2097176
  26.8 0.0 copy-start.3
  26.8 1.0 %copy-done.3 = bf16[512,512]{1,0:T(8,128)(2,1)S(1)} copy-done((bf16[512,512]{1,0:T(8,128)(2,1)S(1)}, bf16[512,512]{1,0:T(8,128)(2,1)}, u32[]{:S(2)}) %copy-start.3) | copy-done | bytes 524312
  27.9 0.0 copy-start.4
  27.9 1.0 %copy-done.4 = bf16[512,512]{1,0:T(8,128)(2,1)S(1)} copy-done((bf16[512,512]{1,0:T(8,128)(2,1)S(1)}, bf16[512,512]{1,0:T(8,128)(2,1)}, u32[]{:S(2)}) %copy-start.4) | copy-done | bytes 524312
  28.9 17.3 %attention_backward.1 = (bf16[2,512,512]{2,1,0:T(8,128)(2,1)S(1)}, bf16[8,2,512,128]{3,2,1,0:T(8,128)(2,1)S(1)}) custom-call(s32[1,8]{1,0:T(1,128)S(1)} %copy-done.5, s32[1,8]{1,0:T(1,128)S(1)} %copy-done.6, bf16[512,1024]{1,0:T(8,128)(2,1)S(1)} %bitcast.6, bf16[512,1024]{1,0:T(8,128)(2,1)S(1)} %bitcast.8, bf16[512,512]{1,0:T(8,128)(2,1)S(1)} %copy-done.3, ...), custom_call_target="tpu_custom_call" | custom-call | tf_op jit(solution)/shard_map/attention_backward/pallas_call | solution.py:583
  46.2 34.8 %reduce_and_pass.1 = (bf16[512,1024]{1,0:T(8,128)(2,1)S(1)}, bf16[2,512,128]{2,1,0:T(8,128)(2,1)S(1)}) custom-call(bf16[2,512,512]{2,1,0:T(8,128)(2,1)S(1)} %get-tuple-element.13.dq_ref, bf16[8,2,512,128]{3,2,1,0:T(8,128)(2,1)S(1)} %get-tuple-element.14.dkv_ref), custom_call_target="tpu_custom_call" | custom-call | tf_op jit(solution)/shard_map/reduce_and_pass/pallas_call | solution.py:357
  81.0 0.7 fusion
  81.7 1.0 %copy.10 = bf16[1,512,1024]{2,1,0:T(8,128)(2,1)} copy(bf16[1,512,1024]{2,1,0:T(8,128)(2,1)S(1)} %bitcast.9) | data formatting | bytes 2097152
Async XLA Ops:
  0.6 24.6 %copy-start.6 = (s32[1,8]{1,0:T(1,128)S(1)}, s32[1,8]{1,0:T(1,128)}, u32[]{:S(2)}) copy-start(s32[1,8]{1,0:T(1,128)} %placing_ref.1) | copy-start | bytes 100
  0.6 24.6 %copy-start.5 = (s32[1,8]{1,0:T(1,128)S(1)}, s32[1,8]{1,0:T(1,128)}, u32[]{:S(2)}) copy-start(s32[1,8]{1,0:T(1,128)} %sizes_ref.1) | copy-start | bytes 100
  0.7 24.6 %copy-start.1 = (bf16[1,512,1024]{2,1,0:T(8,128)(2,1)S(1)}, bf16[1,512,1024]{2,1,0:T(8,128)(2,1)}, u32[]{:S(2)}) copy-start(bf16[1,512,1024]{2,1,0:T(8,128)(2,1)} %param.9) | copy-start | bytes 3145732
  0.7 24.6 %copy-start = (bf16[1,512,1024]{2,1,0:T(8,128)(2,1)S(1)}, bf16[1,512,1024]{2,1,0:T(8,128)(2,1)}, u32[]{:S(2)}) copy-start(bf16[1,512,1024]{2,1,0:T(8,128)(2,1)} %param.6) | copy-start | bytes 3145732
  25.2 1.6 %copy-start.2 = (bf16[8,2,512,128]{3,2,1,0:T(8,128)(2,1)S(1)}, bf16[8,2,512,128]{3,2,1,0:T(8,128)(2,1)}, u32[]{:S(2)}) copy-start(bf16[8,2,512,128]{3,2,1,0:T(8,128)(2,1)} %get-tuple-element.12.kv_ref) | copy-start | bytes 6291460
  26.8 1.0 %copy-start.3 = (bf16[512,512]{1,0:T(8,128)(2,1)S(1)}, bf16[512,512]{1,0:T(8,128)(2,1)}, u32[]{:S(2)}) copy-start(bf16[512,512]{1,0:T(8,128)(2,1)} %get-tuple-element.10.qo_ref) | copy-start | bytes 1572868
  27.9 1.0 %copy-start.4 = (bf16[512,512]{1,0:T(8,128)(2,1)S(1)}, bf16[512,512]{1,0:T(8,128)(2,1)}, u32[]{:S(2)}) copy-start(bf16[512,512]{1,0:T(8,128)(2,1)} %get-tuple-element.11.go_ref) | copy-start | bytes 1572868
where the time goes:
time: 82.4 us; the launch traced here: 82.7 us
  Pallas kernels  76.6 us (93%)
  local copies, waits for them, and re-layouts  5.37 us (7%)
    pallas_call x1, Pallas kernels, reduce_and_pass(): pl.pallas_call(reduce_kernel, out_shape=(jax.ShapeDtypeStruct((rows, 2 *...  34.8 us
    pallas_call x1, Pallas kernels, gather(): pl.pallas_call(gather_kernel, out_shape=(jax.ShapeDtypeStruct((n_ctx, 2)...  24.5 us
    pallas_call x1, Pallas kernels, attention_backward(): pl.pallas_call(attention_kernel, out_shape=(jax.ShapeDtypeStruct((2, rows...  17.3 us
    unnamed x15, local copies, waits for them, and re-layouts  4.65 us

commit v1 on v0

--- a/solution.py
+++ b/solution.py
@@ -57,8 +57,6 @@
     q_ref,
     g_ref,
     kv_ref,
-    qo_ref,
-    go_ref,
     own_sem,
     line_send,
     line_recv,
@@ -68,8 +66,9 @@
     swap_recv,
 ):
     me = lax.axis_index("ctx")
-    chips = kv_ref.shape[0] // 2
-    half = qo_ref.shape[1]
+    head_width = k_ref.shape[1]
+    heads = q_ref.shape[1] // head_width // 2
+    chips = (kv_ref.shape[0] - 2 * heads) // 4
     chip, core = me // 2, me % 2
     twin = chip_device(chip, 1 - core)
     has = (chip < chips - 1, chip > 0)
@@ -79,7 +78,7 @@
 
     sources = (k_ref, v_ref)
     own = [
-        pltpu.make_async_copy(ref, kv_ref.at[me, part], own_sem.at[part])
+        pltpu.make_async_copy(ref, kv_ref.at[2 * me + part], own_sem.at[part])
         for part, ref in enumerate(sources)
     ]
 
@@ -87,7 +86,7 @@
         return 2 * (chip - step if way == 0 else chip + step) + core
 
     def along(way, step, hop, part):
-        place = kv_ref.at[shard_at(way, step), part]
+        place = kv_ref.at[2 * shard_at(way, step) + part]
         return remote(
             sources[part] if hop == 0 and step == 0 else place,
             place,
@@ -97,7 +96,7 @@
         )
 
     def across(way, step, part):
-        place = kv_ref.at[shard_at(way, step), part]
+        place = kv_ref.at[2 * shard_at(way, step) + part]
         return remote(
             sources[part] if step == 0 else place,
             place,
@@ -119,11 +118,19 @@
     for part in range(2):
         across(0, 0, part).start()
         own[part].start()
-    lanes = pl.ds(pl.multiple_of((1 - core) * half, half), half)
-    swaps = [
-        remote(q_ref.at[:, lanes], qo_ref, swap_send.at[0], swap_recv.at[0], twin),
-        remote(g_ref.at[:, lanes], go_ref, swap_send.at[1], swap_recv.at[1], twin),
-    ]
+    swaps = []
+    for index, ref in enumerate((q_ref, g_ref)):
+        for h in range(heads):
+            first = pl.multiple_of(((1 - core) * heads + h) * head_width, head_width)
+            swaps.append(
+                remote(
+                    ref.at[:, pl.ds(first, head_width)],
+                    kv_ref.at[4 * chips + index * heads + h],
+                    swap_send.at[index, h],
+                    swap_recv.at[index, h],
+                    twin,
+                )
+            )
     for copy in swaps:
         copy.start()
     for step in range(1, chips):
@@ -168,24 +175,20 @@
     rows, width = queries.shape
     n_ctx = lax.axis_size("ctx")
     chips = n_ctx // 2
-    half = width // 2
+    heads = width // keys.shape[1] // 2
     return pl.pallas_call(
         gather_kernel,
-        out_shape=(
-            jax.ShapeDtypeStruct((n_ctx, 2) + keys.shape, keys.dtype),
-            jax.ShapeDtypeStruct((rows, half), queries.dtype),
-            jax.ShapeDtypeStruct((rows, half), queries.dtype),
-        ),
+        out_shape=jax.ShapeDtypeStruct((2 * n_ctx + 2 * heads,) + keys.shape, keys.dtype),
         in_specs=[pl.BlockSpec(memory_space=pl.ANY)] * 4,
-        out_specs=(pl.BlockSpec(memory_space=pl.ANY),) * 3,
+        out_specs=pl.BlockSpec(memory_space=pl.ANY),
         scratch_shapes=[
             pltpu.SemaphoreType.DMA((2,)),
             pltpu.SemaphoreType.DMA((2, chips, 2)),
             pltpu.SemaphoreType.DMA((2, chips, 2)),
             pltpu.SemaphoreType.DMA((2, chips, 2)),
             pltpu.SemaphoreType.DMA((2, chips, 2)),
-            pltpu.SemaphoreType.DMA((2,)),
-            pltpu.SemaphoreType.DMA((2,)),
+            pltpu.SemaphoreType.DMA((2, heads)),
+            pltpu.SemaphoreType.DMA((2, heads)),
         ],
         compiler_params=pltpu.CompilerParams(collective_id=0, has_side_effects=True),
         name="gather_blocks",
@@ -246,7 +249,7 @@
             dkv_ref.at[2 * z + 1 - core], twin_ref.at[z], twin_send.at[z], twin_recv.at[z], twin
         )
 
-    for z in order:
+    for z in order[:2]:
         crossing(z).start()
 
     lanes = pl.ds(pl.multiple_of(core * half, half), half)
@@ -262,6 +265,8 @@
 
     for k in range(2):
         query_copy(k, core).start()
+    for z in order[2:]:
+        crossing(z).start()
 
     def passing(way, z, part):
         return remote(
@@ -389,8 +394,6 @@
     placing_ref,
     q_ref,
     g_ref,
-    qo_ref,
-    go_ref,
     kv_ref,
     dq_ref,
     dkv_ref,
@@ -406,11 +409,12 @@
     *rest,
 ):
     low_refs = (rest[:2], rest[2:4])
-    dqt_ref, acc_ref, place_ref = rest[4:]
+    dq_acc_ref, acc_ref, place_ref = rest[4:]
     block = q_ref.shape[0] // 2
-    head_width = kv_ref.shape[3]
+    head_width = kv_ref.shape[2]
     head_count = q_ref.shape[1] // head_width
     n_ctx = placing_ref.shape[1]
+    n_chips = n_ctx // 2
     n_docs = sizes_ref.shape[1]
     heads = head_count // 2
     wide = heads * block
@@ -447,9 +451,8 @@
         @pl.when(owner != core)
         def _():
             for h in range(heads):
-                lanes = slice(h * head_width, (h + 1) * head_width)
-                qs_ref[h * block : (h + 1) * block, :] = qo_ref[rows, lanes]
-                gs_ref[h * block : (h + 1) * block, :] = go_ref[rows, lanes]
+                qs_ref[h * block : (h + 1) * block, :] = kv_ref[4 * n_chips + h, rows, :]
+                gs_ref[h * block : (h + 1) * block, :] = kv_ref[4 * n_chips + heads + h, rows, :]
 
         first = query_block * block
         query_pos = first + lax.broadcasted_iota(jnp.int32, (1, block), 1)
@@ -460,7 +463,7 @@
             strip_first = jnp.where(first >= start, start, strip_first)
         low_block = strip_first // block
         tiles = query_block - low_block + 1
-        dqt_ref[...] = jnp.zeros_like(dqt_ref)
+        dq_acc_ref[...] = jnp.zeros_like(dq_acc_ref)
 
         last_doc = jnp.int32(0)
         for start in starts[1:]:
@@ -472,7 +475,7 @@
         def tile_of(t, part):
             stored = place_ref[low_block + t]
             key_rows = pl.ds(pl.multiple_of(stored % 2 * block, block), block)
-            return kv_ref[stored // 2, part, key_rows, :]
+            return kv_ref[stored // 2 * 2 + part, key_rows, :]
 
         def fold(x, combine):
             return combine(x.reshape(block // 8, 8, block), axis=0)
@@ -539,7 +542,7 @@
                         low_refs[i][1][r : r + 64, lanes] = grad_scores.astype(jnp.bfloat16)
                 acc_ref[stored // 2, 1, key_rows, :] += dot_nn(low_refs[i][0][...], gs_ref[...])
                 acc_ref[stored // 2, 0, key_rows, :] += dot_nn(low_refs[i][1][...], qs_ref[...])
-                dqt_ref[...] += dot_tn(key_tile, low_refs[i][1][...])
+                dq_acc_ref[...] += dot_tn(low_refs[i][1][...], key_tile)
 
         def over_tiles(work):
             def pair(i, carry):
@@ -559,7 +562,7 @@
         over_tiles(backward)
         for h in range(heads):
             dq_ref[owner, rows, h * head_width : (h + 1) * head_width] = (
-                jnp.transpose(dqt_ref[:, h * block : (h + 1) * block]) * scale
+                dq_acc_ref[h * block : (h + 1) * block, :] * scale
             ).astype(jnp.bfloat16)
         return carry
 
@@ -568,11 +571,12 @@
     dkv_ref[:, 1] = acc_ref[:, 1].astype(dkv_ref.dtype)
 
 
-def attention_backward(doc_lengths, assignment, queries, out_grad, queries_other, out_grad_other, kv):
+def attention_backward(doc_lengths, assignment, queries, out_grad, kv):
     rows, width = queries.shape
-    length = kv.shape[0] * rows
+    n_ctx = assignment.shape[1]
+    length = n_ctx * rows
     block = rows // 2
-    head_width = kv.shape[3]
+    head_width = kv.shape[2]
     wide = width // head_width // 2 * block
     most = length // 2
     tiles = most // block + 1
@@ -584,9 +588,9 @@
         attention_kernel,
         out_shape=(
             jax.ShapeDtypeStruct((2, rows, width // 2), jnp.bfloat16),
-            jax.ShapeDtypeStruct(kv.shape, jnp.bfloat16),
+            jax.ShapeDtypeStruct((n_ctx, 2, rows, head_width), jnp.bfloat16),
         ),
-        in_specs=[smem, smem, vmem, vmem, vmem, vmem, vmem],
+        in_specs=[smem, smem, vmem, vmem, vmem],
         out_specs=(vmem, vmem),
         scratch_shapes=[
             pltpu.VMEM((wide, head_width), jnp.bfloat16),
@@ -602,20 +606,18 @@
             pltpu.VMEM((block, wide), jnp.bfloat16),
             pltpu.VMEM((block, wide), jnp.bfloat16),
             pltpu.VMEM((block, wide), jnp.bfloat16),
-            pltpu.VMEM((head_width, wide), jnp.float32),
-            pltpu.VMEM(kv.shape, jnp.float32),
+            pltpu.VMEM((wide, head_width), jnp.float32),
+            pltpu.VMEM((n_ctx, 2, rows, head_width), jnp.float32),
             pltpu.SMEM((2 * assignment.shape[1],), jnp.int32),
         ],
         compiler_params=pltpu.CompilerParams(vmem_limit_bytes=limit),
         name="attention_backward",
-    )(doc_lengths, assignment, queries, out_grad, queries_other, out_grad_other, kv)
+    )(doc_lengths, assignment, queries, out_grad, kv)
 
 
 def local(queries, keys, values, out_grad, doc_lengths, assignment):
-    kv, queries_other, out_grad_other = gather(keys[0], values[0], queries[0], out_grad[0])
-    dq, dkv = attention_backward(
-        doc_lengths, assignment, queries[0], out_grad[0], queries_other, out_grad_other, kv
-    )
+    kv = gather(keys[0], values[0], queries[0], out_grad[0])
+    dq, dkv = attention_backward(doc_lengths, assignment, queries[0], out_grad[0], kv)
     query_in, kv_in = reduce_and_pass(dq, dkv)
     return query_in[None], kv_in[0][None], kv_in[1][None]
 

time: 82.4 us -> 80.7 us (0.979)
  the two profiles are of different devices: /device:TPU:0 before, /device:TPU:16 now
where the time goes in v1:
time: 80.7 us
  Pallas kernels  76.4 us (95%)
  local copies, waits for them, and re-layouts  3.59 us (4%)
    pallas_call x1, Pallas kernels, reduce_and_pass(): pl.pallas_call(reduce_kernel, out_shape=(jax.ShapeDtypeStruct((rows, 2 *...  39.8 us
    pallas_call x1, Pallas kernels, gather(): pl.pallas_call(gather_kernel, out_shape=jax.ShapeDtypeStruct((2 * n_ctx +...  19.5 us
    pallas_call x1, Pallas kernels, attention_backward(): pl.pallas_call(attention_kernel, out_shape=(jax.ShapeDtypeStruct((2, rows...  17 us
    unnamed x11, local copies, waits for them, and re-layouts  2.87 us

profile of v1, /device:TPU:16, one launch (start us, length us, event | category | flops | bytes accessed | tf_op | source)
XLA Modules:
  0.0 80.7 jit_solution(3936074091078621113)
XLA Ops:
  0.6 0.0 copy-start.4
  0.6 0.0 copy-start.3
  0.7 0.0 copy-start.2
  0.7 0.0 copy-start.1
  0.7 19.5 %gather_blocks.1.kv_ref = bf16[24,512,128]{2,1,0:T(8,128)(2,1)} custom-call(bf16[512,128]{1,0:T(8,128)(2,1)} %bitcast.10, bf16[512,128]{1,0:T(8,128)(2,1)} %bitcast.11, bf16[512,1024]{1,0:T(8,128)(2,1)} %bitcast.5, bf16[512,1024]{1,0:T(8,128)(2,1)} %bitcast.7), custom_call_target="tpu_custom_call" | custom-call | tf_op jit(solution)/shard_map/gather_blocks/pallas_call | solution.py:179
  20.2 0.0 copy-done.4
  20.2 0.0 copy-done.3
  20.2 0.0 copy-done.2
  20.2 0.0 copy-done.1
  20.2 0.0 copy-start
  20.2 1.9 %copy-done = bf16[24,512,128]{2,1,0:T(8,128)(2,1)S(1)} copy-done((bf16[24,512,128]{2,1,0:T(8,128)(2,1)S(1)}, bf16[24,512,128]{2,1,0:T(8,128)(2,1)}, u32[]{:S(2)}) %copy-start) | copy-done | bytes 3145752
  22.1 17.0 %attention_backward.1 = (bf16[2,512,512]{2,1,0:T(8,128)(2,1)S(1)}, bf16[8,2,512,128]{3,2,1,0:T(8,128)(2,1)S(1)}) custom-call(s32[1,8]{1,0:T(1,128)S(1)} %copy-done.3, s32[1,8]{1,0:T(1,128)S(1)} %copy-done.4, bf16[512,1024]{1,0:T(8,128)(2,1)S(1)} %bitcast.6, bf16[512,1024]{1,0:T(8,128)(2,1)S(1)} %bitcast.8, bf16[24,512,128]{2,1,0:T(8,128)(2,1)S(1)} %copy-done), custom_call_target="tpu_custom_call" | custom-call | tf_op jit(solution)/shard_map/attention_backward/pallas_call | solution.py:587
  39.2 39.8 %reduce_and_pass.1 = (bf16[512,1024]{1,0:T(8,128)(2,1)S(1)}, bf16[2,512,128]{2,1,0:T(8,128)(2,1)S(1)}) custom-call(bf16[2,512,512]{2,1,0:T(8,128)(2,1)S(1)} %get-tuple-element.7.dq_ref, bf16[8,2,512,128]{3,2,1,0:T(8,128)(2,1)S(1)} %get-tuple-element.8.dkv_ref), custom_call_target="tpu_custom_call" | custom-call | tf_op jit(solution)/shard_map/reduce_and_pass/pallas_call | solution.py:362
  79.0 0.7 fusion
  79.7 1.0 %copy.10 = bf16[1,512,1024]{2,1,0:T(8,128)(2,1)} copy(bf16[1,512,1024]{2,1,0:T(8,128)(2,1)S(1)} %bitcast.9) | data formatting | bytes 2097152
Async XLA Ops:
  0.6 19.5 %copy-start.4 = (s32[1,8]{1,0:T(1,128)S(1)}, s32[1,8]{1,0:T(1,128)}, u32[]{:S(2)}) copy-start(s32[1,8]{1,0:T(1,128)} %placing_ref.1) | copy-start | bytes 100
  0.6 19.5 %copy-start.3 = (s32[1,8]{1,0:T(1,128)S(1)}, s32[1,8]{1,0:T(1,128)}, u32[]{:S(2)}) copy-start(s32[1,8]{1,0:T(1,128)} %sizes_ref.1) | copy-start | bytes 100
  0.7 19.5 %copy-start.2 = (bf16[1,512,1024]{2,1,0:T(8,128)(2,1)S(1)}, bf16[1,512,1024]{2,1,0:T(8,128)(2,1)}, u32[]{:S(2)}) copy-start(bf16[1,512,1024]{2,1,0:T(8,128)(2,1)} %param.9) | copy-start | bytes 3145732
  0.7 19.5 %copy-start.1 = (bf16[1,512,1024]{2,1,0:T(8,128)(2,1)S(1)}, bf16[1,512,1024]{2,1,0:T(8,128)(2,1)}, u32[]{:S(2)}) copy-start(bf16[1,512,1024]{2,1,0:T(8,128)(2,1)} %param.6) | copy-start | bytes 3145732
  20.2 1.9 %copy-start = (bf16[24,512,128]{2,1,0:T(8,128)(2,1)S(1)}, bf16[24,512,128]{2,1,0:T(8,128)(2,1)}, u32[]{:S(2)}) copy-start(bf16[24,512,128]{2,1,0:T(8,128)(2,1)} %gather_blocks.1.kv_ref) | copy-start | bytes 9437188
